TPU v7x, 512 devices: a whole 4x8x8 slice. The times are simulated.
512 devices in a mesh: section: 16 (over y, x_hi), dp: 32 (over z, x_lo, core).
Axes of the slice: x: 4 (x_hi: 2, x_lo: 2; x = x_hi * 2 + x_lo), y: 8, z: 8, core: 2. Of those that a mesh axis runs over, the one named last changes fastest.
Arguments:
- saved_states: bfloat16 [16, 2, 128, 2688], P('section', None, 'dp'), may hold values from -64 to 64
- cotangent_in: bfloat16 [16, 128, 2688], P('section', 'dp'), may hold values from -6 to 6
- lengths: int32 [16], P('section'), may hold values from 16 to 128
- gain: bfloat16 [2688], replicated, may hold values from 0.099609375 to 1.8984375
- up_weight: bfloat16 [2688, 9216], P('section', 'dp'), may hold values from -0.125 to 0.125
- down_weight: bfloat16 [9216, 2688], P('dp', 'section'), may hold values from -0.0625 to 0.0625
Outputs:
- cotangent_out: bfloat16 [16, 128, 2688], P('section', 'dp')
- up_gradient: bfloat16 [2688, 9216], P('section', 'dp')
- down_gradient: bfloat16 [9216, 2688], P('dp', 'section')
- gain_gradient: float32 [2688], replicated
All inputs are finite; a program needn't handle non-finite values.
Results may differ from a plain program's by a relative error of at most 0.024.
Values may be sent and summed in bfloat16 or wider, within the bound.
A program may use at most 64 MiB of HBM per device.

v0:
```python
import math
import jax
import jax.numpy as jnp
from jax import lax
from jax.sharding import PartitionSpec as P

epsilon = 1e-06


def passed_along(block, axis, distance):
    devices = range(lax.axis_size(axis))
    route = [((i - distance) % len(devices), i) for i in devices]
    return lax.ppermute(block, axis, route)


def back_iteration(state, cotangent, gain, up_full, down_full):
    values = state.astype(jnp.float32)
    reciprocal = lax.rsqrt(jnp.mean(values * values, axis=-1, keepdims=True) + epsilon)
    scaled = values * reciprocal
    gain_wide = gain.astype(jnp.float32)
    normed = (scaled * gain_wide).astype(jnp.bfloat16)
    hidden_in = jnp.dot(normed, up_full, preferred_element_type=jnp.float32)
    sigma = jax.nn.sigmoid(hidden_in)
    hidden_out = (hidden_in * sigma).astype(jnp.bfloat16)
    back_out = lax.dot_general(
        cotangent, down_full, (((1,), (1,)), ((), ())), preferred_element_type=jnp.float32
    )
    back_in = (back_out * sigma * (1.0 + hidden_in * (1.0 - sigma))).astype(jnp.bfloat16)
    partial_value = lax.dot_general(
        back_in, up_full, (((1,), (1,)), ((), ())), preferred_element_type=jnp.float32
    )
    back_normed = lax.psum(partial_value.astype(jnp.bfloat16), "dp").astype(jnp.float32)
    rows_scaled, rows_recip, rows_cot = (scaled, reciprocal, cotangent)
    gained = back_normed * gain_wide
    back_state = rows_recip * (
        gained - rows_scaled * jnp.mean(gained * rows_scaled, axis=-1, keepdims=True)
    )
    result = (rows_cot.astype(jnp.float32) + back_state).astype(jnp.bfloat16)
    gain_term = jnp.sum(back_normed * rows_scaled, axis=0)
    return (result, normed, back_in, hidden_out, gain_term)


def hand_over(result):
    moved = passed_along(result, "section", -1)
    return moved


def contract_rows(left, right):
    return lax.dot_general(
        left, right, (((0,), (0,)), ((), ())), preferred_element_type=jnp.float32
    )


def reduce_terms(up_terms, down_terms):
    return (
        lax.psum_scatter(
            up_terms.astype(jnp.bfloat16), "section", scatter_dimension=0, tiled=True
        ).astype(jnp.float32),
        lax.psum_scatter(
            down_terms.astype(jnp.bfloat16), "section", scatter_dimension=1, tiled=True
        ).astype(jnp.float32),
    )


def on_device(saved_states, cotangent_in, lengths, gain, up_weight, down_weight):
    up_full, down_full = (
        lax.all_gather(up_weight, "section", axis=0, tiled=True),
        lax.all_gather(down_weight, "section", axis=1, tiled=True),
    )
    group_states, group_cotangent = (
        lax.all_gather(saved_states, "dp", axis=2, tiled=True),
        lax.all_gather(cotangent_in, "dp", axis=1, tiled=True),
    )
    turns = group_states.shape[1]
    tokens = group_states.shape[2]
    share = saved_states.shape[2]
    member = lax.axis_index("dp")
    positions = lax.broadcasted_iota(jnp.int32, (tokens, 1), 0)
    cotangent = jnp.where(
        positions < lengths[0], group_cotangent[0], jnp.zeros_like(group_cotangent[0])
    )
    scale = 1.0 / math.sqrt(turns * tokens * lax.axis_size("section"))
    gain_total = jnp.zeros((gain.shape[0],), jnp.float32)
    up_total = jnp.zeros(up_full.shape, jnp.float32)
    down_total = jnp.zeros(down_full.shape, jnp.float32)
    result = cotangent
    for turn in range(turns):
        if turn > 0:
            cotangent = hand_over(result)
        result, normed, back_in, hidden_out, gain_term = back_iteration(
            group_states[0, turn], cotangent, gain, up_full, down_full
        )
        gain_total = gain_total + gain_term
        up_total = up_total + contract_rows(normed, back_in)
        down_total = down_total + contract_rows(hidden_out, cotangent)
    up_sum, down_sum = reduce_terms(up_total * scale, down_total * scale)
    gain_sum = lax.psum(gain_total * scale, "section")
    own_rows = lax.dynamic_slice_in_dim(result, member * share, share, 0)[None]
    return (own_rows, up_sum.astype(jnp.bfloat16), down_sum.astype(jnp.bfloat16), gain_sum)


def solution(mesh):
    placed = (
        P("section", None, "dp", None),
        P("section", "dp", None),
        P("section"),
        P(),
        P("section", "dp"),
        P("dp", "section"),
    )
    return jax.shard_map(
        on_device,
        mesh=mesh,
        in_specs=placed,
        out_specs=(P("section", "dp", None), P("section", "dp"), P("dp", "section"), P()),
        check_vma=False,
    )
```

profile of v0, /device:TPU:16, one launch (start us, length us, event | category | flops | bytes accessed | tf_op | source)
XLA Modules:
  0.0 1156.4 jit_solution(15592596476500519794)
XLA Ops:
  7.2 0.0 all-gather.4.cloned.1.call-start
  7.2 1.4 copy.15
  8.6 0.0 all-gather.4.cloned.1.call-update
  8.7 0.0 all-gather.8.cloned.1.call-start
  8.7 0.7 all-gather.8.cloned.1.call-update
  9.4 0.0 all-gather.6.cloned.1.call-start
  9.5 0.7 all-gather.6.cloned.1.call-update
  10.2 0.0 all-reduce.5.cloned.1.call-start
  10.2 0.7 convert_element_type.71
  10.9 0.8 copy.14
  12.3 47.3 %all_gather.12 = bf16[1,128,2688]{2,0,1:T(2,128)(2,1)} all-gather(bf16[1,4,2688]{2,0,1:T(2,128)(2,1)S(1)} %copy.14), channel_id=1, replica_groups=mesh['section'=16,'dp'=32] {'dp'}, dimensions={1}, use_global_device_ids=true | all-gather | bytes 709632 | tf_op jit(solution)/shard_map/all_gather | solution.py:72
  59.6 22.9 %all-gather.4.cloned.1.call-done = bf16[1,2,128,2688]{3,1,0,2:T(2,128)(2,1)} async-done(((bf16[1,2,4,2688]{3,1,0,2:T(2,128)(2,1)}), bf16[1,2,128,2688]{3,1,0,2:T(2,128)(2,1)}) %all-gather.4.cloned.1.call-update) | async-done | bytes 1376272 | tf_op jit(solution)/shard_map/all_gather | solution.py:71
  82.5 5.2 fusion.36
  87.8 0.2 fusion.16
  88.0 86.3 %all-gather.8.cloned.1.call-done = bf16[2688,288]{1,0:T(8,128)(2,1)} async-done(((bf16[168,288]{1,0:T(8,128)(2,1)}), bf16[2688,288]{1,0:T(8,128)(2,1)}) %all-gather.8.cloned.1.call-update) | async-done | bytes 1548304 | tf_op jit(solution)/shard_map/all_gather | solution.py:67
  174.3 2.4 fusion.25
  176.7 88.4 %all-gather.6.cloned.1.call-done = bf16[288,2688]{0,1:T(8,128)(2,1)} async-done(((bf16[288,168]{0,1:T(8,128)(2,1)}), bf16[288,2688]{0,1:T(8,128)(2,1)}) %all-gather.6.cloned.1.call-update) | async-done | bytes 1548304 | tf_op jit(solution)/shard_map/all_gather | solution.py:68
  265.2 2.9 fusion.20
  268.1 1.7 convolution_convert_fusion.1
  269.7 0.0 all-reduce.5.cloned.1.call-update
  269.7 0.0 all-reduce.7.cloned.1.call-start
  269.8 224.5 %all-reduce.5.cloned.1.call-done = bf16[128,2688]{1,0:T(8,128)(2,1)} async-done(((bf16[128,2688]{1,0:T(8,128)(2,1)}), bf16[128,2688]{1,0:T(8,128)(2,1)}) %all-reduce.5.cloned.1.call-update) | async-done | bytes 688144 | tf_op jit(solution)/shard_map/psum | solution.py:32
  494.2 1.7 fusion.15
  496.0 1.7 fusion.11
  497.8 4.9 collective-permute-start
  502.6 0.2 fusion.17
  502.9 0.8 fusion.22
  503.8 14.3 %collective-permute-done = bf16[128,2688]{1,0:T(8,128)(2,1)S(1)} collective-permute-done((bf16[128,2688]{1,0:T(8,128)(2,1)S(1)}, bf16[128,2688]{1,0:T(8,128)(2,1)S(1)}, u32[]{:S(2)}, u32[]{:S(2)}) %collective-permute-start) | collective-permute-done | bytes 688160 | tf_op jit(solution)/shard_map/ppermute | solution.py:13
  518.1 0.8 fusion.21
  518.9 1.7 convolution_convert_fusion
  520.6 0.0 all-reduce.7.cloned.1.call-update
  520.6 0.0 reduce-scatter.7.cloned.1.call-start
  520.7 1.7 fusion.23
  522.4 2.2 fusion.2
  524.5 0.0 reduce-scatter.7.cloned.1.call-update
  524.6 0.2 reduce-scatter.9.cloned.1.call-start
  524.8 1.1 copy-done.2
  525.9 0.8 fusion.27
  526.7 2.1 fusion.3
  528.8 0.0 reduce-scatter.9.cloned.1.call-update
  528.8 0.1 dynamic-slice.5
  528.9 218.3 %all-reduce.7.cloned.1.call-done = bf16[128,2688]{1,0:T(8,128)(2,1)} async-done(((bf16[128,2688]{1,0:T(8,128)(2,1)}), bf16[128,2688]{1,0:T(8,128)(2,1)}) %all-reduce.7.cloned.1.call-update) | async-done | bytes 688144 | tf_op jit(solution)/shard_map/psum | solution.py:32
  747.2 2.5 fusion.12
  749.7 0.1 dynamic-slice.4
  749.8 72.7 %psum.23 = f32[2688]{0:T(1024)} all-reduce(f32[2688]{0:T(1024)S(1)} %add_multiply_fusion), channel_id=1, replica_groups=mesh['section'=16,'dp'=32] {'section'}, use_global_device_ids=true, to_apply=%region_10.11 | all-reduce | flops 2688 | bytes 21504 | tf_op jit(solution)/shard_map/psum | solution.py:97
  822.5 1.6 fusion.33
  824.1 125.8 %reduce-scatter.7.cloned.1.call-done = bf16[168,288]{1,0:T(8,128)(2,1)} async-done(((bf16[2688,288]{1,0:T(8,128)(2,1)}), bf16[168,288]{1,0:T(8,128)(2,1)}) %reduce-scatter.7.cloned.1.call-update) | async-done | bytes 96784
  949.9 199.7 %reduce-scatter.9.cloned.1.call-done = bf16[288,168]{0,1:T(8,128)(2,1)} async-done(((bf16[288,2688]{0,1:T(8,128)(2,1)}), bf16[288,168]{0,1:T(8,128)(2,1)}) %reduce-scatter.9.cloned.1.call-update) | async-done | bytes 96784
  (29 shorter events, 0.1 us)
Async XLA Ops:
  7.2 75.4 %all-gather.4.cloned.1.call-start = ((), (), s32[]{:S(2)}) async-start(), calls=%async_computation.2 | async-start | bytes 1419264 | tf_op jit(solution)/shard_map/all_gather | solution.py:71
  8.7 165.6 %all-gather.8.cloned.1.call-start = ((), (), s32[]{:S(2)}) async-start(), calls=%async_computation.4 | async-start | bytes 2193408 | tf_op jit(solution)/shard_map/all_gather | solution.py:67
  9.4 255.7 %all-gather.6.cloned.1.call-start = ((), (), s32[]{:S(2)}) async-start(), calls=%async_computation.3 | async-start | bytes 2193408 | tf_op jit(solution)/shard_map/all_gather | solution.py:68
  10.2 484.1 %all-reduce.5.cloned.1.call-start = ((), (), s32[]{:S(2)}) async-start(), calls=%async_computation.5 | async-start | bytes 1376256 | tf_op jit(solution)/shard_map/psum | solution.py:32
  176.7 91.3 %copy-start.9 = (f32[128,288]{0,1:T(8,128)}, f32[128,288]{0,1:T(8,128)S(1)}, u32[]{:S(2)}) copy-start(f32[128,288]{0,1:T(8,128)S(1)} %fusion.25) | copy-start | bytes 442372
  176.7 91.3 %copy-start = (bf16[2688,288]{1,0:T(8,128)(2,1)S(1)}, bf16[2688,288]{1,0:T(8,128)(2,1)}, u32[]{:S(2)}) copy-start(bf16[2688,288]{1,0:T(8,128)(2,1)} %all-gather.8.cloned.1.call-done) | copy-start | bytes 4644868
  268.0 1.7 copy-start.11
  269.7 477.4 %all-reduce.7.cloned.1.call-start = ((), (), s32[]{:S(2)}) async-start(), calls=%async_computation.6 | async-start | bytes 1376256 | tf_op jit(solution)/shard_map/psum | solution.py:32
  494.2 1.8 copy-start.1
  496.0 6.6 copy-start.3
  497.8 20.3 %collective-permute-start = (bf16[128,2688]{1,0:T(8,128)(2,1)S(1)}, bf16[128,2688]{1,0:T(8,128)(2,1)S(1)}, u32[]{:S(2)}, u32[]{:S(2)}) collective-permute-start(bf16[128,2688]{1,0:T(8,128)(2,1)S(1)} %fusion.11), channel_id=1, source_target_pairs={{32,0},{64,32},{96,64},{128,96},{160,128},{192,160},{224,192},{256... | collective-permute-start | bytes 2064392 | tf_op jit(solution)/shard_map/ppermute | solution.py:13
  502.9 15.2 %copy-start.8 = (bf16[288,2688]{0,1:T(8,128)(2,1)S(1)}, bf16[288,2688]{0,1:T(8,128)(2,1)}, u32[]{:S(2)}) copy-start(bf16[288,2688]{0,1:T(8,128)(2,1)} %all-gather.6.cloned.1.call-done) | copy-start | bytes 4644868
  503.8 15.1 %copy-start.6 = (f32[128,288]{0,1:T(8,128)}, f32[128,288]{0,1:T(8,128)S(1)}, u32[]{:S(2)}) copy-start(f32[128,288]{0,1:T(8,128)S(1)} %fusion.22) | copy-start | bytes 442372
  518.1 0.9 copy-start.4
  520.6 429.2 %reduce-scatter.7.cloned.1.call-start = ((), (), s32[]{:S(2)}) async-start(), calls=%async_computation.7 | async-start | bytes 2193408
  524.5 1.3 copy-start.2
  524.5 1.3 copy-start.10
  524.6 2.1 copy-start.5
  524.6 2.1 copy-start.7
  524.6 625.0 %reduce-scatter.9.cloned.1.call-start = ((), (), s32[]{:S(2)}) async-start(), calls=%async_computation.8 | async-start | bytes 2193408
Sparse Core Ops, SparseCore 0:
  10.7 71.7 all-gather.3
  85.7 88.5 all-gather.7
  177.5 87.6 all-gather.5
  269.9 224.3 all-reduce.4
  520.8 226.3 all-reduce.6
  752.1 197.6 reduce-scatter.6
  955.0 194.5 reduce-scatter.8
where the time goes:
time: 1160 us
  waiting for transfers between devices  982 us (85%)
  blocking collectives  120 us (10%)
  matrix products  17.1 us (1%)
  between operations  15 us (1%)
    psum x2, waiting for transfers between devices, back_iteration(): lax.psum(partial_value.astype(jnp.bfloat16), 'dp').astype(jnp.float32)  443 us
    unnamed x9, waiting for transfers between devices  327 us
    all_gather x1, waiting for transfers between devices, on_device(): lax.all_gather(down_weight, 'section', axis=1, tiled=True)  88.4 us
    all_gather x1, waiting for transfers between devices, on_device(): lax.all_gather(up_weight, 'section', axis=0, tiled=True)  86.3 us
    psum x1, blocking collectives, on_device(): gain_sum = lax.psum(gain_total * scale, 'section')  72.7 us
    all_gather x1, blocking collectives, on_device(): lax.all_gather(cotangent_in, 'dp', axis=1, tiled=True)  47.3 us
  transfers between devices with their start and end apart: 8, of which 8 were waited for; matrix products, arithmetic and copies ran while one was open for 2% of the time, Pallas kernels for 0%

commit v1 on v0

--- a/solution.py
+++ b/solution.py
@@ -29,7 +29,9 @@
     partial_value = lax.dot_general(
         back_in, up_full, (((1,), (1,)), ((), ())), preferred_element_type=jnp.float32
     )
-    back_normed = lax.psum(partial_value.astype(jnp.bfloat16), "dp").astype(jnp.float32)
+    back_normed = jnp.sum(lax.all_gather(partial_value.astype(jnp.bfloat16), "dp"), axis=0).astype(
+        jnp.float32
+    )
     rows_scaled, rows_recip, rows_cot = (scaled, reciprocal, cotangent)
     gained = back_normed * gain_wide
     back_state = rows_recip * (

time: 1160 us -> 975 us (0.84)
  waiting for transfers between devices: 982 us -> 777 us
  other arithmetic: 8.83 us -> 29.9 us
    psum x2 -> x0, waiting for transfers between devices: 443 us -> none  [back_iteration(): lax.psum(partial_value.astype(jnp.bfloat16), 'dp').astype(jnp.float32)]
    all_gather x0 -> x2, waiting for transfers between devices: none -> 250 us  [back_iteration(): lax.all_gather(partial_value.astype(jnp.bfloat16), 'dp')]
    reduce_sum x0 -> x2, other arithmetic: none -> 24.5 us  [back_iteration(): jnp.sum(lax.all_gather(partial_value.astype(jnp.bfloat16), 'dp'), axis=0)]
    unnamed x9, waiting for transfers between devices: 327 us -> 315 us
  transfers between devices with their start and end apart: 8 -> 8, of which waited for: 8 -> 8; matrix products, arithmetic and copies ran while one was open for 2% -> 3% of each run, Pallas kernels for 0% -> 0%
where the time goes in v1:
time: 975 us; the launch traced here: 974 us
  waiting for transfers between devices  777 us (80%)
  blocking collectives  120 us (12%)
  other arithmetic  29.9 us (3%)
  matrix products  17.8 us (2%)
  between operations  15 us (2%)
    unnamed x9, waiting for transfers between devices  315 us
    all_gather x2, waiting for transfers between devices, back_iteration(): lax.all_gather(partial_value.astype(jnp.bfloat16), 'dp')  250 us
    all_gather x1, waiting for transfers between devices, on_device(): lax.all_gather(down_weight, 'section', axis=1, tiled=True)  88.4 us
    all_gather x1, waiting for transfers between devices, on_device(): lax.all_gather(up_weight, 'section', axis=0, tiled=True)  86.3 us
    psum x1, blocking collectives, on_device(): gain_sum = lax.psum(gain_total * scale, 'section')  73 us
    all_gather x1, blocking collectives, on_device(): lax.all_gather(cotangent_in, 'dp', axis=1, tiled=True)  47.2 us
    reduce_sum x2, other arithmetic, back_iteration(): jnp.sum(lax.all_gather(partial_value.astype(jnp.bfloat16), 'dp'), axis=0)  24.5 us
    all_gather x1, waiting for transfers between devices, on_device(): lax.all_gather(saved_states, 'dp', axis=2, tiled=True)  23 us
  transfers between devices with their start and end apart: 8, of which 8 were waited for; matrix products, arithmetic and copies ran while one was open for 3% of the time, Pallas kernels for 0%

profile of v1, /device:TPU:16, one launch (start us, length us, event | category | flops | bytes accessed | tf_op | source)
XLA Modules:
  0.0 974.0 jit_solution(17856963264292540458)
XLA Ops:
  7.2 0.0 all-gather.8.cloned.1.call-start
  7.2 1.4 copy.15
  8.7 0.0 all-gather.12.cloned.1.call-start
  8.7 0.7 all-gather.12.cloned.1.call-update
  9.4 0.0 all-gather.10.cloned.1.call-start
  9.5 0.7 all-gather.10.cloned.1.call-update
  10.2 0.0 all-gather.14.cloned.1.call-start
  10.8 0.7 convert_element_type.75
  11.5 0.8 copy.14
  12.3 47.2 %all_gather.24 = bf16[1,128,2688]{2,0,1:T(2,128)(2,1)} all-gather(bf16[1,4,2688]{2,0,1:T(2,128)(2,1)S(1)} %copy.14), channel_id=1, replica_groups=mesh['section'=16,'dp'=32] {'dp'}, dimensions={1}, use_global_device_ids=true | all-gather | bytes 709632 | tf_op jit(solution)/shard_map/all_gather | solution.py:74
  59.5 23.0 %all-gather.8.cloned.1.call-done = bf16[1,2,128,2688]{3,1,0,2:T(2,128)(2,1)} async-done(((bf16[1,2,4,2688]{3,1,0,2:T(2,128)(2,1)}), bf16[1,2,128,2688]{3,1,0,2:T(2,128)(2,1)}) %all-gather.8.cloned.1.call-update) | async-done | bytes 1376272 | tf_op jit(solution)/shard_map/all_gather | solution.py:73
  82.5 5.2 fusion.36
  87.8 0.2 fusion.16
  88.0 86.3 %all-gather.12.cloned.1.call-done = bf16[2688,288]{1,0:T(8,128)(2,1)} async-done(((bf16[168,288]{1,0:T(8,128)(2,1)}), bf16[2688,288]{1,0:T(8,128)(2,1)}) %all-gather.12.cloned.1.call-update) | async-done | bytes 1548304 | tf_op jit(solution)/shard_map/all_gather | solution.py:69
  174.3 2.4 fusion.25
  176.7 88.4 %all-gather.10.cloned.1.call-done = bf16[288,2688]{0,1:T(8,128)(2,1)} async-done(((bf16[288,168]{0,1:T(8,128)(2,1)}), bf16[288,2688]{0,1:T(8,128)(2,1)}) %all-gather.10.cloned.1.call-update) | async-done | bytes 1548304 | tf_op jit(solution)/shard_map/all_gather | solution.py:70
  265.2 2.9 fusion.20
  268.1 1.7 convolution_convert_fusion.1
  269.7 0.0 all-gather.14.cloned.1.call-update
  269.8 0.0 all-gather.16.cloned.1.call-start
  269.8 127.6 %all-gather.14.cloned.1.call-done = bf16[4096,2688]{1,0:T(8,128)(2,1)} async-done(((bf16[128,2688]{1,0:T(8,128)(2,1)}), bf16[4096,2688]{1,0:T(8,128)(2,1)}) %all-gather.14.cloned.1.call-update) | async-done | bytes 22020112 | tf_op jit(solution)/shard_map/all_gather | solution.py:32
  397.4 12.3 %reduce_sum.79 = bf16[128,2688]{1,0:T(8,128)(2,1)S(1)} reduce(bf16[32,128,2688]{2,1,0:T(8,128)(2,1)} %bitcast.40, bf16[]{:T(256)} %constant.10.clone.1), dimensions={0}, to_apply=%region_1.2 | reduce | flops 10665984 | bytes 22708226 | tf_op jit(solution)/shard_map/reduce_sum | solution.py:32
  409.7 0.5 fusion.15
  410.2 0.8 copy-done.1
  411.0 0.6 fusion.11
  411.6 4.9 collective-permute-start
  416.5 0.2 fusion.17
  416.7 0.8 fusion.22
  417.6 15.0 %collective-permute-done = bf16[128,2688]{1,0:T(8,128)(2,1)S(1)} collective-permute-done((bf16[128,2688]{1,0:T(8,128)(2,1)S(1)}, bf16[128,2688]{1,0:T(8,128)(2,1)S(1)}, u32[]{:S(2)}, u32[]{:S(2)}) %collective-permute-start) | collective-permute-done | bytes 688160 | tf_op jit(solution)/shard_map/ppermute | solution.py:13
  432.6 0.8 fusion.21
  433.4 0.1 copy-done.3
  433.5 1.7 convolution_convert_fusion
  435.2 0.0 reduce-scatter.9.cloned.1.call-start
  435.3 2.3 fusion.27
  437.6 2.2 fusion.3
  439.8 0.2 reduce-scatter.7.cloned.1.call-start
  440.0 0.6 copy-done.10
  440.6 0.8 fusion.23
  441.4 2.2 fusion.2
  443.7 0.1 dynamic-slice.5
  443.7 121.9 %all-gather.16.cloned.1.call-done = bf16[4096,2688]{1,0:T(8,128)(2,1)} async-done(((bf16[128,2688]{1,0:T(8,128)(2,1)}), bf16[4096,2688]{1,0:T(8,128)(2,1)}) %all-gather.16.cloned.1.call-update) | async-done | bytes 22020112 | tf_op jit(solution)/shard_map/all_gather | solution.py:32
  565.7 12.3 %reduce_sum.82 = bf16[128,2688]{1,0:T(8,128)(2,1)S(1)} reduce(bf16[32,128,2688]{2,1,0:T(8,128)(2,1)} %bitcast.39, bf16[]{:T(256)} %constant.10.clone.1), dimensions={0}, to_apply=%region_4.5 | reduce | flops 10665984 | bytes 22708226 | tf_op jit(solution)/shard_map/reduce_sum | solution.py:32
  578.0 1.4 fusion.12
  579.4 0.1 dynamic-slice.4
  579.5 73.0 %psum.7 = f32[2688]{0:T(1024)} all-reduce(f32[2688]{0:T(1024)S(1)} %add_multiply_fusion), channel_id=1, replica_groups=mesh['section'=16,'dp'=32] {'section'}, use_global_device_ids=true, to_apply=%region_10.11 | all-reduce | flops 2688 | bytes 21504 | tf_op jit(solution)/shard_map/psum | solution.py:99
  652.5 1.6 fusion.33
  654.1 113.1 %reduce-scatter.9.cloned.1.call-done = bf16[288,168]{0,1:T(8,128)(2,1)} async-done(((bf16[288,2688]{0,1:T(8,128)(2,1)}), bf16[288,168]{0,1:T(8,128)(2,1)}) %reduce-scatter.9.cloned.1.call-update) | async-done | bytes 96784
  767.2 199.9 %reduce-scatter.7.cloned.1.call-done = bf16[168,288]{1,0:T(8,128)(2,1)} async-done(((bf16[2688,288]{1,0:T(8,128)(2,1)}), bf16[168,288]{1,0:T(8,128)(2,1)}) %reduce-scatter.7.cloned.1.call-update) | async-done | bytes 96784
  (29 shorter events, 0.1 us)
Async XLA Ops:
  7.2 75.4 %all-gather.8.cloned.1.call-start = ((), (), s32[]{:S(2)}) async-start(), calls=%async_computation.2 | async-start | bytes 1419264 | tf_op jit(solution)/shard_map/all_gather | solution.py:73
  8.7 165.6 %all-gather.12.cloned.1.call-start = ((), (), s32[]{:S(2)}) async-start(), calls=%async_computation.4 | async-start | bytes 2193408 | tf_op jit(solution)/shard_map/all_gather | solution.py:69
  9.4 255.7 %all-gather.10.cloned.1.call-start = ((), (), s32[]{:S(2)}) async-start(), calls=%async_computation.3 | async-start | bytes 2193408 | tf_op jit(solution)/shard_map/all_gather | solution.py:70
  10.2 387.3 %all-gather.14.cloned.1.call-start = ((), (), s32[]{:S(2)}) async-start(), calls=%async_computation.5 | async-start | bytes 22708224 | tf_op jit(solution)/shard_map/all_gather | solution.py:32
  176.7 91.3 %copy-start.8 = (f32[128,288]{0,1:T(8,128)}, f32[128,288]{0,1:T(8,128)S(1)}, u32[]{:S(2)}) copy-start(f32[128,288]{0,1:T(8,128)S(1)} %fusion.25) | copy-start | bytes 442372
  176.7 91.3 %copy-start = (bf16[2688,288]{1,0:T(8,128)(2,1)S(1)}, bf16[2688,288]{1,0:T(8,128)(2,1)}, u32[]{:S(2)}) copy-start(bf16[2688,288]{1,0:T(8,128)(2,1)} %all-gather.12.cloned.1.call-done) | copy-start | bytes 4644868
  268.0 1.7 copy-start.9
  269.8 295.9 %all-gather.16.cloned.1.call-start = ((), (), s32[]{:S(2)}) async-start(), calls=%async_computation.6 | async-start | bytes 22708224 | tf_op jit(solution)/shard_map/all_gather | solution.py:32
  409.7 1.3 copy-start.1
  411.0 5.4 copy-start.2
  411.6 21.0 %collective-permute-start = (bf16[128,2688]{1,0:T(8,128)(2,1)S(1)}, bf16[128,2688]{1,0:T(8,128)(2,1)S(1)}, u32[]{:S(2)}, u32[]{:S(2)}) collective-permute-start(bf16[128,2688]{1,0:T(8,128)(2,1)S(1)} %fusion.11), channel_id=1, source_target_pairs={{32,0},{64,32},{96,64},{128,96},{160,128},{192,160},{224,192},{256... | collective-permute-start | bytes 2064392 | tf_op jit(solution)/shard_map/ppermute | solution.py:13
  416.7 15.9 %copy-start.7 = (bf16[288,2688]{0,1:T(8,128)(2,1)S(1)}, bf16[288,2688]{0,1:T(8,128)(2,1)}, u32[]{:S(2)}) copy-start(bf16[288,2688]{0,1:T(8,128)(2,1)} %all-gather.10.cloned.1.call-done) | copy-start | bytes 4644868
  417.6 15.9 %copy-start.5 = (f32[128,288]{0,1:T(8,128)}, f32[128,288]{0,1:T(8,128)S(1)}, u32[]{:S(2)}) copy-start(f32[128,288]{0,1:T(8,128)S(1)} %fusion.22) | copy-start | bytes 442372
  432.6 0.9 copy-start.3
  435.2 2.4 copy-start.4
  435.2 2.4 copy-start.6
  435.2 332.0 %reduce-scatter.9.cloned.1.call-start = ((), (), s32[]{:S(2)}) async-start(), calls=%async_computation.8 | async-start | bytes 2193408
  439.8 0.9 copy-start.10
  439.8 527.3 %reduce-scatter.7.cloned.1.call-start = ((), (), s32[]{:S(2)}) async-start(), calls=%async_computation.7 | async-start | bytes 2193408
Sparse Core Ops, SparseCore 0:
  10.7 71.7 all-gather.7
  85.7 88.5 all-gather.11
  177.5 87.6 all-gather.9
  269.9 127.5 all-gather.13
  435.3 130.3 all-gather.15
  570.7 196.4 reduce-scatter.8
  772.3 194.7 reduce-scatter.6
